TPU v7x, 32 devices: a whole 2x2x4 slice. The times are simulated.
32 devices in a mesh: group: 2 (over x), seq: 4 (over y, core), tp: 4 (over z).
Axes of the slice: x: 2, y: 2, z: 4, core: 2. Of those that a mesh axis runs over, the one named last changes fastest.
Arguments:
- queries: bfloat16 [4096, 4096], P(('group', 'seq'), 'tp'), parts along dimension 0, may hold values from -32 to 32
- key_value: bfloat16 [4096, 2, 2048], P(('group', 'seq'), None, 'tp'), parts along dimension 0, may hold values from -32 to 32
- window_cache: bfloat16 [2048, 2, 2048], P('group', None, 'tp'), parts along dimension 0, may hold values from -5 to 5
- span_start: int32 [2], P('group'), parts along dimension 0, may hold values from 1024 to 30720
- hidden: bfloat16 [4096, 21504], P(('group', 'seq'), 'tp'), parts along dimension 0, may hold values from -6 to 6
- down_codes: int32 [21504, 2688], P('tp', 'seq'), may hold values from 0 to 15
- down_scales: int32 [168, 2688], P('tp', 'seq'), may hold values from 1 to 15
- out_weight: bfloat16 [4096, 2688], P('tp', 'seq'), may hold values from -0.375 to 0.375
Outputs:
- layer_update: bfloat16 [4096, 2688], P(('group', 'seq', 'tp')), parts along dimension 0
There are 2 independent parts, one for each index of `group`. A program takes and returns all parts, laid end to end along the dimension named above; an argument that names none is the same for every part. Nothing has to cross between parts.
All inputs are finite; a program needn't handle non-finite values.
Results may differ from a plain program's by a relative error of at most 0.02.
Values may be sent and summed in bfloat16 or wider, within the bound.
No kernel may reach another device: no remote copies, remote signals or barrier semaphores. Data moves between devices by JAX's collectives and lax.ppermute only.
A program may use at most 192 MiB of HBM per device.

v0:
```python
import jax
import jax.numpy as jnp
import numpy as np
from jax import lax
from jax.sharding import PartitionSpec as P

HD = 128
WINDOW = 1024
GROUP = 128


ROPE_BASE = 10000.0
SCORE_SCALE = 168.0 ** (-0.5)
CODE_STEP = 2.0 ** (-14)
INV_ROOT = 1344.0 ** (-0.5)


def shifted(value, axis, steps):
    count = lax.axis_size(axis)
    first, last = (max(0, -steps), min(count, count - steps))
    return lax.ppermute(value, axis, [(source, source + steps) for source in range(first, last)])


def swapped(x, axis, stride):
    return lax.ppermute(x, axis, [(i, i ^ 1 << stride) for i in range(lax.axis_size(axis))])


def bit_total(value_now):
    return (value_now & 1) + (value_now >> 1 & 1) + (value_now >> 2 & 1)


def build_tables():
    prime_order = 167
    residues = set((value_now * value_now % prime_order for value_now in range(1, prime_order)))
    legendre = [0] + [1 if value_now in residues else -1 for value_now in range(1, prime_order)]
    paley_table = np.eye(prime_order + 1)
    paley_table[0, 1:] += 1.0
    paley_table[1:, 0] -= 1.0
    for row_index in range(prime_order):
        for col_index in range(prime_order):
            paley_table[row_index + 1, col_index + 1] += legendre[
                (col_index - row_index) % prime_order
            ]
    sylvester = np.array(
        [
            [(-1.0) ** bit_total(left_bit & right_bit) for right_bit in range(8)]
            for left_bit in range(8)
        ]
    )
    return (paley_table, sylvester)


def rotary(values, cosine, sine_part):
    half_dim = values.shape[-1] // 2
    first_half = values[..., :half_dim]
    second_half = values[..., half_dim:]
    return jnp.concatenate(
        [
            first_half * cosine - second_half * sine_part,
            second_half * cosine + first_half * sine_part,
        ],
        axis=-1,
    )


def section_pairs(blocks_now, section_level):
    row_count, block_count, width_cols = blocks_now.shape
    paired = blocks_now.reshape(
        row_count, block_count >> section_level + 1, 2, 1 << section_level, width_cols
    ).astype(jnp.float32)
    upper_half = paired[:, :, 0]
    lower_half = paired[:, :, 1]
    mixed = jnp.stack([upper_half + lower_half, upper_half - lower_half], axis=2)
    return mixed.astype(jnp.bfloat16).reshape(row_count, block_count, width_cols)


def per_device(
    queries, key_value, window_cache, span_start, hidden, down_codes, down_scales, out_weight
):
    tok_rows = queries.shape[0]
    tp_count = lax.axis_size("tp")
    seq_index = lax.axis_index("seq")
    tp_index = lax.axis_index("tp")
    heads_dev = queries.shape[1] // HD
    kv_dev = key_value.shape[2] // HD
    group_size = heads_dev // kv_dev
    first_pos = span_start[0]
    positions = first_pos + seq_index * tok_rows + jnp.arange(tok_rows, dtype=jnp.int32)
    inv_freq = ROPE_BASE ** (-(2.0 * jnp.arange(HD // 2, dtype=jnp.float32)) / HD)
    angles = positions.astype(jnp.float32)[:, None] * inv_freq[None, :]
    cosine = jnp.cos(angles)[:, None, :]
    sine_part = jnp.sin(angles)[:, None, :]
    query_rot = rotary(
        queries.reshape(tok_rows, heads_dev, HD).astype(jnp.float32), cosine, sine_part
    ).astype(jnp.bfloat16)
    key_rot = rotary(
        key_value[:, 0].reshape(tok_rows, kv_dev, HD).astype(jnp.float32), cosine, sine_part
    ).astype(jnp.bfloat16)
    own_pairs = jnp.stack([key_rot.reshape(tok_rows, kv_dev * HD), key_value[:, 1]], axis=1)
    reach_blocks = WINDOW // tok_rows
    earlier = []
    moving = own_pairs
    for hop_count in range(reach_blocks):
        moving = shifted(moving, "seq", 1)
        earlier.insert(0, moving)
    halo_rows = jnp.concatenate(earlier, axis=0)
    doubled = jnp.concatenate([window_cache, window_cache], axis=0)
    ordered = lax.dynamic_slice_in_dim(doubled, first_pos % WINDOW, WINDOW, 0)
    padded_cache = jnp.concatenate([ordered, jnp.zeros_like(ordered)], axis=0)
    from_cache = lax.dynamic_slice_in_dim(
        padded_cache, jnp.minimum(seq_index * tok_rows, WINDOW), WINDOW, 0
    )
    halo_rows = halo_rows + from_cache
    all_rows = jnp.concatenate([halo_rows, own_pairs], axis=0)
    key_count = all_rows.shape[0]
    key_rows = all_rows[:, 0].reshape(key_count, kv_dev, HD)
    value_rows = all_rows[:, 1].reshape(key_count, kv_dev, HD)
    grouped = query_rot.reshape(tok_rows, kv_dev, group_size, HD)
    scores = (
        jnp.einsum("qkgd,skd->kgqs", grouped, key_rows, preferred_element_type=jnp.float32)
        * SCORE_SCALE
    )
    query_ids = jnp.arange(tok_rows)[:, None]
    key_ids = jnp.arange(key_count)[None, :]
    allowed = (key_ids > query_ids) & (key_ids <= query_ids + WINDOW)
    scores = jnp.where(allowed, scores, -jnp.inf)
    top_score = jnp.max(scores, axis=-1, keepdims=True)
    weights_soft = jnp.exp(scores - top_score)
    weights_soft = (weights_soft / jnp.sum(weights_soft, axis=-1, keepdims=True)).astype(
        jnp.bfloat16
    )
    attended = jnp.einsum(
        "kgqs,skd->qkgd", weights_soft, value_rows, preferred_element_type=jnp.float32
    )
    attended = attended.astype(jnp.bfloat16).reshape(tok_rows, heads_dev * HD)
    paley_np, sylvester_np = build_tables()
    paley_table = jnp.asarray(paley_np, dtype=jnp.bfloat16)
    sylvester = jnp.asarray(sylvester_np, dtype=jnp.float32)
    local_blocks = hidden.shape[1] // 1344
    local_levels = local_blocks.bit_length() - 1
    parts_now = hidden.reshape(tok_rows, local_blocks, 8, 168)
    mixed = jnp.einsum("nbac,cd->nbad", parts_now, paley_table, preferred_element_type=jnp.float32)
    mixed = (
        jnp.einsum("nbad,ae->nbed", mixed, sylvester, precision=lax.Precision.HIGHEST) * INV_ROOT
    )
    blocks_now = mixed.reshape(tok_rows, local_blocks, 1344).astype(jnp.bfloat16)
    for section_level in range(local_levels):
        blocks_now = section_pairs(blocks_now, section_level)
    for bit_index in range(tp_count.bit_length() - 1):
        partner = swapped(blocks_now, "tp", bit_index)
        high_side = jnp.right_shift(tp_index, bit_index) % 2
        own_values = blocks_now.astype(jnp.float32)
        other_values = partner.astype(jnp.float32)
        blocks_now = jnp.where(
            high_side == 0, own_values + other_values, other_values - own_values
        ).astype(jnp.bfloat16)
    rotated = blocks_now.reshape(tok_rows, local_blocks * 1344)
    joined = jnp.concatenate([rotated, attended], axis=1)
    group_count = down_scales.shape[0]
    col_count = down_codes.shape[1]
    down_weight = (
        (down_codes.reshape(group_count, GROUP, col_count) - 8) * down_scales[:, None, :]
    ).astype(jnp.float32) * CODE_STEP
    down_rows = down_weight.astype(jnp.bfloat16).reshape(group_count * GROUP, col_count)
    stacked = jnp.concatenate([down_rows, out_weight], axis=0)
    partials = jnp.dot(
        joined,
        lax.all_gather(stacked, "seq", axis=1, tiled=True),
        preferred_element_type=jnp.float32,
    )
    layer_update = lax.psum_scatter(
        partials.astype(jnp.bfloat16), "tp", scatter_dimension=0, tiled=True
    )
    return layer_update


def solution(mesh):
    return jax.shard_map(
        per_device,
        mesh=mesh,
        in_specs=(
            P(("group", "seq"), "tp"),
            P(("group", "seq"), None, "tp"),
            P("group", None, "tp"),
            P("group"),
            P(("group", "seq"), "tp"),
            P("tp", "seq"),
            P("tp", "seq"),
            P("tp", "seq"),
        ),
        out_specs=P(("group", "seq", "tp"), None),
        check_vma=False,
    )
```

profile of v0, /device:TPU:0, one launch (start us, length us, event | category | flops | bytes accessed | tf_op | source)
XLA Modules:
  0.0 548.5 jit_solution(3099437337702410601)
XLA Ops:
  6.5 1.1 copy.50
  7.6 4.5 mul.147
  12.2 9.4 %fusion.4 = bf16[5376,672]{0,1:T(8,128)(2,1)S(1)} fusion(s32[84,8,42,128]{3,2,1,0:T(8,128)S(1)} %bitcast.77, s32[5376,672]{0,1:T(8,128)} %param.15), kind=kLoop, calls=%fused_computation.8 | loop fusion | flops 18063360 | bytes 36126720 | tf_op jit(solution)/shard_map/convert_element_type | solution.py:164
  21.6 3.7 pad_maximum_fusion
  25.3 0.0 all-gather.2.cloned.1.call-update
  25.3 0.2 reduce-scatter.2.cloned.1.call-start
  25.5 8.3 %copy.33 = bf16[512,5376]{0,1:T(8,128)(2,1)} copy(bf16[512,5376]{1,0:T(8,128)(2,1)} %param.14) | data formatting | bytes 11010048 | tf_op args[4]
  33.8 5.6 %convolution_bitcast_fusion = f32[512,4,8,168]{0,3,2,1:T(8,128)S(1)} fusion(bf16[168,168,1,1]{0,1,3,2:T(8,128)(2,1)S(1)} %copy-done.7, bf16[512,4,8,168]{0,3,2,1:T(8,128)(2,1)} %bitcast.79), kind=kOutput, calls=%fused_computation.43 | convolution fusion | flops 924844032 | bytes 16571520 | tf_op jit(solution)/shard_map/nbac,cd->nbad/dot_general | solution.py:142
  39.4 16.7 %convert_bitcast_fusion = f32[512,4,8,168]{0,2,3,1:T(8,128)} fusion(f32[8,8,1,1]{0,1,3,2:T(8,128)S(1)} %copy-done.8, f32[512,4,8,168]{0,3,2,1:T(8,128)S(1)} %convolution_bitcast_fusion), kind=kOutput, calls=%fused_computation.23 | convolution fusion | flops 272498688 | bytes 22020352 | tf_op jit(solution)/shard_map/nbad,ae->nbed/dot_general | solution.py:144
  56.2 11.1 %copy.35 = f32[512,4,8,168]{0,3,2,1:T(8,128)S(1)} copy(f32[512,4,8,168]{0,2,3,1:T(8,128)} %convert_bitcast_fusion) | data formatting | bytes 22020096 | tf_op jit(solution)/shard_map/convert_element_type | solution.py:70
  67.2 4.1 fusion.27
  71.3 3.3 maximum_convert_fusion
  74.6 1.9 add_convert_fusion
  76.5 0.5 pad_maximum_fusion.1
  77.0 2.7 copy.37
  79.8 3.3 collective-permute-start
  83.8 2.5 fusion.45
  86.2 0.1 copy_convert_fusion
  86.3 0.3 copy.58
  86.7 2.3 copy.60
  89.1 0.5 multiply_cosine_fusion
  89.6 0.2 subtract_convert_fusion.3
  89.8 0.1 pad_maximum_fusion.2
  89.9 2.5 collective-permute-start.2
  92.4 109.7 %collective-permute-done = bf16[512,4,1344]{0,2,1:T(8,128)(2,1)} collective-permute-done((bf16[512,4,1344]{0,2,1:T(8,128)(2,1)}, bf16[512,4,1344]{0,2,1:T(8,128)(2,1)}, u32[]{:S(2)}, u32[]{:S(2)}) %collective-permute-start) | collective-permute-done | bytes 5505056 | tf_op jit(solution)/shard_map/ppermute | solution.py:25
  202.1 8.6 %fusion.10 = bf16[512,4,1344]{0,2,1:T(8,128)(2,1)} fusion(bf16[512,4,1344]{0,2,1:T(8,128)(2,1)} %collective-permute-done, pred[]{:T(512)S(6)} %eq.11, bf16[512,1,2,2,1344]{0,4,3,2,1:T(8,128)(2,1)} %copy.37), kind=kLoop, calls=%fused_computation.18 | loop fusion | flops 16515072 | bytes 16515073 | tf_op jit(solution)/shard_map/convert_element_type | solution.py:156
  210.7 2.8 collective-permute-start.1
  213.4 0.2 convert_bitcast_fusion.1
  213.7 0.5 copy.63
  214.2 2.7 fusion.44
  216.9 2.2 collective-permute-start.3
  219.1 0.1 copy.45
  219.3 0.8 copy.47
  220.1 4.7 copy.42
  224.9 2.1 fusion.30
  227.0 0.0 copy-done.1
  227.1 1.8 subtract_convert_fusion.2
  228.9 1.6 fusion.26
  230.5 2.7 fusion.29
  233.2 0.2 maximum_maximum_fusion
  233.4 0.2 fusion.43
  233.7 12.0 %fusion.32 = f32[4,1536,512,2]{2,1,3,0:T(8,128)} fusion(bf16[1536,4,128,1]{0,2,3,1:T(8,128)(2,1)S(1)} %bitcast.81, bf16[512,4,2,64]{3,0,2,1:T(8,128)(2,1)S(1)} %bitcast.88, bf16[512,4,2,64]{3,0,2,1:T(8,128)(2,1)S(1)} %bitcast.86), kind=kOutput, calls=%fused_computation.62 | convolution fusion | flops 1612709888 | bytes 27787264 | tf_op jit(solution)/shard_map/qkgd,skd->kgqs/dot_general | solution.py:120
  245.7 10.3 %fusion.46 = f32[4,2,512]{2,1,0:T(2,128)S(1)} fusion(pred[512,1536]{0,1:T(8,128)(4,1)} %fusion.26, bf16[1536,4,128,1]{0,2,3,1:T(8,128)(2,1)S(1)} %bitcast.82, bf16[512,4,2,64]{3,0,2,1:T(8,128)(2,1)} %bitcast.89, bf16[512,4,2,64]{3,0,2,1:T(8,128)(2,1)} %bitcast.87), kind=kOutput, calls=%fused_computation.76 | convolution fusion | flops 1637877248 | bytes 3424256 | tf_op jit(solution)/shard_map/sub | solution.py:128
  256.0 13.2 %fusion.31 = bf16[4,128,2,512]{3,1,2,0:T(8,128)(2,1)S(1)} fusion(bf16[1536,4,128,1]{0,2,3,1:T(8,128)(2,1)S(1)} %bitcast.91, f32[4,2,512]{2,1,0:T(2,128)S(1)} %fusion.46, f32[4,1536,512,2]{2,1,3,0:T(8,128)} %fusion.32, pred[512,1536]{0,1:T(8,128)(4,1)} %fusion.26), kind=kOutput, calls=%fused_computation.53 | convolution fusion | flops 1642599936 | bytes 28590080 | tf_op jit(solution)/shard_map/kgqs,skd->qkgd/dot_general | solution.py:132
  269.2 180.5 %collective-permute-done.1 = bf16[512,4,1344]{0,2,1:T(8,128)(2,1)} collective-permute-done((bf16[512,4,1344]{0,2,1:T(8,128)(2,1)}, bf16[512,4,1344]{0,2,1:T(8,128)(2,1)}, u32[]{:S(2)}, u32[]{:S(2)}) %collective-permute-start.1) | collective-permute-done | bytes 5505056 | tf_op jit(solution)/shard_map/ppermute | solution.py:25
  449.7 8.6 %fusion.12 = bf16[512,4,1344]{0,2,1:T(8,128)(2,1)} fusion(bf16[512,4,1344]{0,2,1:T(8,128)(2,1)} %collective-permute-done.1, bf16[512,4,1344]{0,2,1:T(8,128)(2,1)} %fusion.10, pred[]{:T(512)S(6)} %eq.10), kind=kLoop, calls=%fused_computation.20 | loop fusion | flops 16515072 | bytes 16515073 | tf_op jit(solution)/shard_map/convert_element_type | solution.py:156
  458.3 27.9 %fusion.19 = bf16[512,2688]{1,0:T(8,128)(2,1)} fusion(bf16[6400,2688]{0,1:T(8,128)(2,1)} %all-gather.2.cloned.1.call-done, bf16[512,1024]{0,1:T(8,128)(2,1)S(1)} %bitcast.92, bf16[512,5376]{0,1:T(8,128)(2,1)} %bitcast.83), kind=kOutput, calls=%fused_computation.38 | convolution fusion | flops 17630560256 | bytes 43712512 | tf_op jit(solution)/shard_map/dot_general | solution.py:166
  486.3 55.1 %reduce-scatter.2.cloned.1.call-done = bf16[128,2688]{1,0:T(8,128)(2,1)} async-done(((bf16[512,2688]{1,0:T(8,128)(2,1)}), bf16[128,2688]{1,0:T(8,128)(2,1)}) %reduce-scatter.2.cloned.1.call-update) | async-done | bytes 688144 | tf_op jit(solution)/shard_map/reduce_scatter | solution.py:171
  (26 shorter events, 0.1 us)
Async XLA Ops:
  6.5 451.8 %all-gather.2.cloned.1.call-start = ((), (), s32[]{:S(2)}) async-start(), calls=%async_computation.1 | async-start | bytes 43008000 | tf_op jit(solution)/shard_map/all_gather | solution.py:168
  12.2 9.4 %copy-start.5 = (bf16[1024,672]{0,1:T(8,128)(2,1)S(1)}, bf16[1024,672]{0,1:T(8,128)(2,1)}, u32[]{:S(2)}) copy-start(bf16[1024,672]{0,1:T(8,128)(2,1)} %param.17) | copy-start | bytes 4128772
  25.3 8.5 %copy-start.7 = (bf16[168,168,1,1]{0,1,3,2:T(8,128)(2,1)S(1)}, bf16[168,168,1,1]{0,1,3,2:T(8,128)(2,1)}, u32[]{:S(2)}) copy-start(bf16[168,168,1,1]{0,1,3,2:T(8,128)(2,1)} %constant.73) | copy-start | bytes 169348
  25.3 516.1 %reduce-scatter.2.cloned.1.call-start = ((), (), s32[]{:S(2)}) async-start(), calls=%async_computation.2 | async-start | bytes 3440640 | tf_op jit(solution)/shard_map/reduce_scatter | solution.py:171
  33.8 5.6 %copy-start.8 = (f32[8,8,1,1]{0,1,3,2:T(8,128)S(1)}, f32[8,8,1,1]{0,1,3,2:T(8,128)}, u32[]{:S(2)}) copy-start(f32[8,8,1,1]{0,1,3,2:T(8,128)} %constant.74) | copy-start | bytes 772
  77.0 6.7 %copy-start.4 = (bf16[512,2,512]{2,1,0:T(2,128)(2,1)S(1)}, bf16[512,2,512]{2,1,0:T(2,128)(2,1)}, u32[]{:S(2)}) copy-start(bf16[512,2,512]{2,1,0:T(2,128)(2,1)} %param.11) | copy-start | bytes 3145732
  79.8 122.3 %collective-permute-start = (bf16[512,4,1344]{0,2,1:T(8,128)(2,1)}, bf16[512,4,1344]{0,2,1:T(8,128)(2,1)}, u32[]{:S(2)}, u32[]{:S(2)}) collective-permute-start(bf16[512,4,1344]{0,2,1:T(8,128)(2,1)} %bitcast.11), channel_id=1, source_target_pairs={{0,1},{1,0},{2,3},{3,2},{4,5},{5,4},{6,7},{7,6},{8,9},{9,8},{10,11... | collective-permute-start | bytes 16515080 | tf_op jit(solution)/shard_map/ppermute | solution.py:25
  89.9 127.0 %collective-permute-start.2 = (bf16[512,2,512]{0,2,1:T(8,128)(2,1)S(1)}, bf16[512,2,512]{0,2,1:T(8,128)(2,1)}, u32[]{:S(2)}, u32[]{:S(2)}) collective-permute-start(bf16[512,2,512]{0,2,1:T(8,128)(2,1)S(1)} %pad_maximum_fusion.2), channel_id=1, source_target_pairs={{0,4},{4,8},{8,12},{1,5},{5,9},{9,13},{2,6},{6,10},{10,14},{3,7},{... | collective-permute-start | bytes 3145736 | tf_op jit(solution)/shard_map/ppermute | solution.py:21
  92.4 121.0 %copy-start.6 = (bf16[512,1024]{1,0:T(8,128)(2,1)S(1)}, bf16[512,1024]{1,0:T(8,128)(2,1)}, u32[]{:S(2)}) copy-start(bf16[512,1024]{1,0:T(8,128)(2,1)} %param.10) | copy-start | bytes 3145732
  210.7 239.0 %collective-permute-start.1 = (bf16[512,4,1344]{0,2,1:T(8,128)(2,1)}, bf16[512,4,1344]{0,2,1:T(8,128)(2,1)}, u32[]{:S(2)}, u32[]{:S(2)}) collective-permute-start(bf16[512,4,1344]{0,2,1:T(8,128)(2,1)} %fusion.10), channel_id=1, source_target_pairs={{0,2},{1,3},{2,0},{3,1},{4,6},{5,7},{6,4},{7,5},{8,10},{9,11},{10,... | collective-permute-start | bytes 16515080 | tf_op jit(solution)/shard_map/ppermute | solution.py:25
  216.9 13.6 %collective-permute-start.3 = (bf16[512,2,512]{0,2,1:T(8,128)(2,1)}, bf16[512,2,512]{0,2,1:T(8,128)(2,1)}, u32[]{:S(2)}, u32[]{:S(2)}) collective-permute-start(bf16[512,2,512]{0,2,1:T(8,128)(2,1)} %collective-permute-done.2), channel_id=1, source_target_pairs={{0,4},{4,8},{8,12},{1,5},{5,9},{9,13},{2,6},{6,10},{10,14},{3,7},{... | collective-permute-start | bytes 3145736 | tf_op jit(solution)/shard_map/ppermute | solution.py:21
  224.8 2.2 copy-start
  224.9 2.2 copy-start.1
  228.8 4.8 copy-start.2
  228.8 4.8 copy-start.3
Sparse Core Ops, SparseCore 0:
  25.4 228.7 all-gather.1
  486.4 54.9 reduce-scatter.1
where the time goes:
time: 552 us; the launch traced here: 548 us
  waiting for transfers between devices  345 us (62%)
  matrix products  85.8 us (16%)
  other arithmetic  49.7 us (9%)
  local copies, waits for them, and re-layouts  42 us (8%)
  between operations  14.6 us (3%)
  starting transfers between devices  11 us (2%)
    ppermute x2, waiting for transfers between devices, swapped(): lax.ppermute(x, axis, [(i, i ^ 1 << stride) for i in range(lax.axis_size(...  290 us
    reduce_scatter x1, waiting for transfers between devices, per_device(): lax.psum_scatter(partials.astype(jnp.bfloat16), 'tp', scatter_dimension=0...  55.1 us
    dot_general x1, matrix products, per_device(): jnp.dot(joined, lax.all_gather(stacked, 'seq', axis=1, tiled=True), prefe...  27.9 us
    convert_element_type x2, other arithmetic, per_device(): blocks_now = jnp.where(high_side == 0, own_values + other_values, other_v...  17.2 us
    unnamed x23, local copies, waits for them, and re-layouts  17 us
    dot_general x1, matrix products, per_device(): jnp.einsum('nbad,ae->nbed', mixed, sylvester, precision=lax.Precision.HIG...  16.7 us
    dot_general x1, matrix products, per_device(): jnp.einsum('kgqs,skd->qkgd', weights_soft, value_rows, preferred_element_...  13.2 us
    dot_general x1, matrix products, per_device(): jnp.einsum('qkgd,skd->kgqs', grouped, key_rows, preferred_element_type=jn...  12 us
  transfers between devices with their start and end apart: 6, of which 3 were waited for; matrix products, arithmetic and copies ran while one was open for 24% of the time, Pallas kernels for 0%

commit v1 on v0

--- a/solution.py
+++ b/solution.py
@@ -2,6 +2,8 @@
 import jax.numpy as jnp
 import numpy as np
 from jax import lax
+from jax.experimental import pallas as pl
+from jax.experimental.pallas import tpu as pltpu
 from jax.sharding import PartitionSpec as P
 
 HD = 128
@@ -174,9 +176,269 @@
     return layer_update
 
 
+BLOCK = 1344
+PADDED = 1408
+
+
+def fits(mesh):
+    return dict(mesh.shape) == {"group": 2, "seq": 4, "tp": 4}
+
+
+def mix_tables():
+    paley_np, sylvester_np = build_tables()
+    mix_np = np.kron(sylvester_np, paley_np)
+    low = np.zeros((PADDED, PADDED), np.float32)
+    high = np.zeros((PADDED, PADDED), np.float32)
+    low[:BLOCK, :BLOCK] = mix_np
+    high[PADDED - BLOCK :, :BLOCK] = mix_np
+    return jnp.asarray(np.stack([low, high]), dtype=jnp.bfloat16)
+
+
+def mix_kernel(hidden_ref, table_ref, out_ref):
+    gap = PADDED - BLOCK
+    pair = 2 * BLOCK
+
+    def product(first, table):
+        return jnp.dot(
+            hidden_ref[:, first : first + PADDED],
+            table_ref[table],
+            preferred_element_type=jnp.float32,
+        )
+
+    sums, differences = [], []
+    for half in range(2):
+        even = product(half * pair, 0)
+        odd = product(half * pair + BLOCK - gap, 1)
+        sums.append(even + odd)
+        differences.append(even - odd)
+    for half in range(2):
+        if half == 0:
+            even, odd = sums[0] + sums[1], differences[0] + differences[1]
+        else:
+            even, odd = sums[0] - sums[1], differences[0] - differences[1]
+        even, odd = even * INV_ROOT, pltpu.roll(odd * INV_ROOT, gap, 1)
+        first, edge = half * pair, BLOCK - gap
+        out_ref[:, first : first + edge] = even[:, :edge].astype(jnp.bfloat16)
+        out_ref[:, first + edge : first + PADDED] = (even[:, edge:] + odd[:, : 2 * gap]).astype(
+            jnp.bfloat16
+        )
+        out_ref[:, first + PADDED : first + pair] = odd[:, 2 * gap :].astype(jnp.bfloat16)
+
+
+def mix_hidden(hidden):
+    rows, width = hidden.shape
+    step = 256
+    return pl.pallas_call(
+        mix_kernel,
+        grid=(rows // step,),
+        in_specs=[
+            pl.BlockSpec((step, width), lambda i: (i, 0)),
+            pl.BlockSpec((2, PADDED, PADDED), lambda i: (0, 0, 0)),
+        ],
+        out_specs=pl.BlockSpec((step, width), lambda i: (i, 0)),
+        out_shape=jax.ShapeDtypeStruct((rows, width), jnp.bfloat16),
+        compiler_params=pltpu.CompilerParams(vmem_limit_bytes=56 << 20),
+        cost_estimate=pl.CostEstimate(
+            flops=2 * rows * width * PADDED, bytes_accessed=4 * rows * width, transcendentals=0
+        ),
+    )(hidden, mix_tables())
+
+
+CHUNKS = ((0, 256), (256, 256), (512, 160))
+
+
+def dequant_kernel(half_ref, codes_ref, scales_ref, *out_refs):
+    row = half_ref[0] * pl.num_programs(0) + pl.program_id(0)
+    weight = ((codes_ref[...] - 8) * scales_ref[pl.ds(row, 1), :]).astype(jnp.float32) * CODE_STEP
+    for (first, size), out_ref in zip(CHUNKS, out_refs):
+        part = weight[:, first : first + size]
+        extra = -size % 128
+        if extra:
+            part = jnp.concatenate([part, jnp.zeros((GROUP, extra), jnp.float32)], axis=1)
+        out_ref[...] = part.T[:size].astype(jnp.bfloat16)
+
+
+def dequant(half_id, codes, scales):
+    rows, cols = codes.shape
+    steps = rows // 2 // GROUP
+    return pl.pallas_call(
+        dequant_kernel,
+        grid_spec=pltpu.PrefetchScalarGridSpec(
+            num_scalar_prefetch=1,
+            grid=(steps,),
+            in_specs=[
+                pl.BlockSpec((GROUP, cols), lambda i, half: (half[0] * steps + i, 0)),
+                pl.BlockSpec(scales.shape, lambda i, half: (0, 0)),
+            ],
+            out_specs=[pl.BlockSpec((size, GROUP), lambda i, half: (0, i)) for _, size in CHUNKS],
+        ),
+        out_shape=[jax.ShapeDtypeStruct((size, rows // 2), jnp.bfloat16) for _, size in CHUNKS],
+        cost_estimate=pl.CostEstimate(
+            flops=2 * rows * cols, bytes_accessed=4 * rows * cols, transcendentals=0
+        ),
+    )(half_id, codes, scales)
+
+
+NT = (((1,), (1,)), ((), ()))
+
+
+def project_kernel(half_ref, *refs):
+    (own_a, own_b, far_a, far_b, own_attn, far_attn) = refs[:6]
+    weights = refs[6:12]
+    out_ref = refs[12]
+    size = weights[0].shape[0]
+    rows_a = jnp.concatenate([own_a[...], far_a[...]], axis=0)
+    rows_b = jnp.concatenate([own_b[...], far_b[...]], axis=0)
+    rows_c = jnp.concatenate([own_attn[...], far_attn[...]], axis=0)
+    for core in range(2):
+        part_a, part_b, part_c = weights[3 * core : 3 * core + 3]
+        total = lax.dot_general(rows_a, part_a[...], NT, preferred_element_type=jnp.float32)
+        total += lax.dot_general(rows_b, part_b[...], NT, preferred_element_type=jnp.float32)
+        total += jnp.dot(rows_c, part_c[...], preferred_element_type=jnp.float32)[:, :size]
+        out_ref[core] = total.astype(jnp.bfloat16)
+
+
+def project(half_id, own, far, own_attn, far_attn, weights, chunk):
+    first, size = CHUNKS[chunk]
+    rows, width = own.shape
+    half = width // 2
+    heads = own_attn.shape[1]
+    step = rows // 4
+    column = first // 256
+    row_specs = [
+        pl.BlockSpec((step, half), lambda i, h: (i, h[0])),
+        pl.BlockSpec((step, half), lambda i, h: (i, 1 - h[0])),
+    ]
+    attn_spec = pl.BlockSpec((step, heads), lambda i, h: (i, 0))
+    weight_spec = pl.BlockSpec((size, half), lambda i, h: (0, 0))
+    side_spec = pl.BlockSpec((heads, 256), lambda i, h: (0, column))
+    return pl.pallas_call(
+        project_kernel,
+        grid_spec=pltpu.PrefetchScalarGridSpec(
+            num_scalar_prefetch=1,
+            grid=(4,),
+            in_specs=row_specs * 2 + [attn_spec] * 2 + [weight_spec, weight_spec, side_spec] * 2,
+            out_specs=pl.BlockSpec((2, 2 * step, size), lambda i, h: (0, i, 0)),
+        ),
+        out_shape=jax.ShapeDtypeStruct((2, 2 * rows, size), jnp.bfloat16),
+        compiler_params=pltpu.CompilerParams(vmem_limit_bytes=56 << 20),
+        cost_estimate=pl.CostEstimate(
+            flops=2 * 2 * rows * (width + heads) * 2 * size,
+            bytes_accessed=2 * (2 * rows * (width + heads) + 2 * size * (width + heads)),
+            transcendentals=0,
+        ),
+    )(half_id, own, own, far, far, own_attn, far_attn, *weights)
+
+
+def attend(queries, key_value, window_cache, first_pos):
+    tok_rows = queries.shape[0]
+    seq_index = lax.axis_index("seq")
+    heads_dev = queries.shape[1] // HD
+    kv_dev = key_value.shape[2] // HD
+    group_size = heads_dev // kv_dev
+    positions = first_pos + seq_index * tok_rows + jnp.arange(tok_rows, dtype=jnp.int32)
+    inv_freq = ROPE_BASE ** (-(2.0 * jnp.arange(HD // 2, dtype=jnp.float32)) / HD)
+    angles = positions.astype(jnp.float32)[:, None] * inv_freq[None, :]
+    cosine = jnp.cos(angles)[:, None, :]
+    sine_part = jnp.sin(angles)[:, None, :]
+    query_rot = rotary(
+        queries.reshape(tok_rows, heads_dev, HD).astype(jnp.float32), cosine, sine_part
+    ).astype(jnp.bfloat16)
+    key_rot = rotary(
+        key_value[:, 0].reshape(tok_rows, kv_dev, HD).astype(jnp.float32), cosine, sine_part
+    ).astype(jnp.bfloat16)
+    own_pairs = jnp.stack([key_rot.reshape(tok_rows, kv_dev * HD), key_value[:, 1]], axis=1)
+    earlier = []
+    moving = own_pairs
+    for hop_count in range(WINDOW // tok_rows):
+        moving = shifted(moving, "seq", 1)
+        earlier.insert(0, moving)
+    halo_rows = jnp.concatenate(earlier, axis=0)
+    doubled = jnp.concatenate([window_cache, window_cache], axis=0)
+    ordered = lax.dynamic_slice_in_dim(doubled, first_pos % WINDOW, WINDOW, 0)
+    padded_cache = jnp.concatenate([ordered, jnp.zeros_like(ordered)], axis=0)
+    from_cache = lax.dynamic_slice_in_dim(
+        padded_cache, jnp.minimum(seq_index * tok_rows, WINDOW), WINDOW, 0
+    )
+    halo_rows = halo_rows + from_cache
+    all_rows = jnp.concatenate([halo_rows, own_pairs], axis=0)
+    key_count = all_rows.shape[0]
+    key_rows = all_rows[:, 0].reshape(key_count, kv_dev, HD)
+    value_rows = all_rows[:, 1].reshape(key_count, kv_dev, HD)
+    grouped = query_rot.reshape(tok_rows, kv_dev, group_size, HD)
+    scores = (
+        jnp.einsum("qkgd,skd->kgqs", grouped, key_rows, preferred_element_type=jnp.float32)
+        * SCORE_SCALE
+    )
+    query_ids = jnp.arange(tok_rows)[:, None]
+    key_ids = jnp.arange(key_count)[None, :]
+    allowed = (key_ids > query_ids) & (key_ids <= query_ids + WINDOW)
+    scores = jnp.where(allowed, scores, -jnp.inf)
+    top_score = jnp.max(scores, axis=-1, keepdims=True)
+    weights_soft = jnp.exp(scores - top_score)
+    weights_soft = (weights_soft / jnp.sum(weights_soft, axis=-1, keepdims=True)).astype(
+        jnp.bfloat16
+    )
+    attended = jnp.einsum(
+        "kgqs,skd->qkgd", weights_soft, value_rows, preferred_element_type=jnp.float32
+    )
+    return attended.astype(jnp.bfloat16).reshape(tok_rows, heads_dev * HD)
+
+
+def flipped(value, axis, bit):
+    return lax.ppermute(value, axis, [(i, i ^ bit) for i in range(lax.axis_size(axis))])
+
+
+def level_step(value, bit):
+    partner = flipped(value, "tp", bit).astype(jnp.float32)
+    own = value.astype(jnp.float32)
+    own = jnp.where(lax.axis_index("tp") & bit == 0, own, -own)
+    return (own + partner).astype(jnp.bfloat16)
+
+
+def planned(
+    queries, key_value, window_cache, span_start, hidden, down_codes, down_scales, out_weight
+):
+    half_id = lax.axis_index("group").reshape(1)
+    seq_index = lax.axis_index("seq")
+    core = seq_index & 1
+    side = seq_index >> 1
+    chunks = dequant(half_id, down_codes, down_scales)
+    rotated = mix_hidden(hidden)
+    far_rotated = flipped(rotated, "seq", 2)
+    attended = attend(queries, key_value, window_cache, span_start[0])
+    far_attended = flipped(attended, "seq", 2)
+    near_out = flipped(out_weight, "seq", 1)
+    reduced = []
+    for chunk, piece in enumerate(chunks):
+        for bit in (2, 1) if chunk == 0 else (1, 2):
+            piece = level_step(piece, bit)
+        across = flipped(piece, "group", 1)
+        near_piece = flipped(piece, "seq", 1)
+        near_across = flipped(across, "seq", 1)
+        partial = project(
+            half_id,
+            rotated,
+            far_rotated,
+            attended,
+            far_attended,
+            [piece, across, out_weight, near_piece, near_across, near_out],
+            chunk,
+        )
+        reduced.append(lax.psum_scatter(partial, "tp", scatter_dimension=1, tiled=True))
+    kept = queries.shape[0] // lax.axis_size("tp")
+    own_side = jnp.concatenate([part[:, :kept] for part in reduced], axis=2)
+    far_side = flipped(jnp.concatenate([part[:, kept:] for part in reduced], axis=2), "seq", 2)
+    own_side = jnp.where(core == 0, own_side, own_side[::-1])
+    far_side = jnp.where(core == 0, far_side, far_side[::-1])
+    first = jnp.where(side == 0, own_side, far_side)
+    second = jnp.where(side == 0, far_side, own_side)
+    return jnp.concatenate([first[0], first[1], second[0], second[1]], axis=1)
+
+
 def solution(mesh):
     return jax.shard_map(
-        per_device,
+        planned if fits(mesh) else per_device,
         mesh=mesh,
         in_specs=(
             P(("group", "seq"), "tp"),

time: 552 us -> 435 us (0.79)
  waiting for transfers between devices: 345 us -> 175 us
  Pallas kernels: 0 us -> 69.4 us
  matrix products: 85.8 us -> 37.6 us
  starting transfers between devices: 11 us -> 56.5 us
  other arithmetic: 49.7 us -> 27.9 us
  local copies, waits for them, and re-layouts: 42 us -> 50.3 us
    ppermute x2 -> x19, waiting for transfers between devices: 290 us -> 151 us  [flipped(): lax.ppermute(value, axis, [(i, i ^ bit) for i in range(lax.axis_size(axis...]
    pallas_call x0 -> x5, Pallas kernels: none -> 69.4 us  [the longest x3 38.7 us: project(): pl.pallas_call(project_kernel, grid_spec=pltpu.PrefetchScalarGridSpec(num...]
    dot_general x5 -> x2, matrix products: 75.5 us -> 27.4 us  [the longest x1 13.9 us: attend(): jnp.einsum('kgqs,skd->qkgd', weights_soft, value_rows, preferred_element_...]
    ppermute x2 -> x19, starting transfers between devices: 6.09 us -> 51.3 us  [flipped(): lax.ppermute(value, axis, [(i, i ^ bit) for i in range(lax.axis_size(axis...]
    reduce_scatter x1 -> x3, waiting for transfers between devices: 55.1 us -> 24.3 us  [planned(): lax.psum_scatter(partial, 'tp', scatter_dimension=1, tiled=True)]
    unnamed x23 -> x37, local copies, waits for them, and re-layouts: 17 us -> 31.5 us
    convert_element_type x6 -> x8, other arithmetic: 30 us -> 15.5 us  [the longest x6 15.4 us: level_step(): return (own + partner).astype(jnp.bfloat16)]
    convert_element_type x2 -> x1, local copies, waits for them, and re-layouts: 11.4 us -> 0.33 us  [attend(): key_value[:, 0].reshape(tok_rows, kv_dev, HD).astype(jnp.float32)]
  transfers between devices with their start and end apart: 6 -> 24, of which waited for: 3 -> 9; matrix products, arithmetic and copies ran while one was open for 24% -> 23% of each run, Pallas kernels for 0% -> 16%
where the time goes in v1:
time: 435 us; the launch traced here: 431 us
  waiting for transfers between devices  175 us (40%)
  Pallas kernels  69.4 us (16%)
  starting transfers between devices  56.5 us (13%)
  local copies, waits for them, and re-layouts  50.3 us (12%)
  matrix products  37.6 us (9%)
  other arithmetic  27.9 us (6%)
  between operations  14.6 us (3%)
    ppermute x19, waiting for transfers between devices, flipped(): lax.ppermute(value, axis, [(i, i ^ bit) for i in range(lax.axis_size(axis...  151 us
    ppermute x19, starting transfers between devices, flipped(): lax.ppermute(value, axis, [(i, i ^ bit) for i in range(lax.axis_size(axis...  51.3 us
    pallas_call x3, Pallas kernels, project(): pl.pallas_call(project_kernel, grid_spec=pltpu.PrefetchScalarGridSpec(num...  38.7 us
    unnamed x37, local copies, waits for them, and re-layouts  31.5 us
    reduce_scatter x3, waiting for transfers between devices, planned(): lax.psum_scatter(partial, 'tp', scatter_dimension=1, tiled=True)  24.3 us
    pallas_call x1, Pallas kernels, mix_hidden(): pl.pallas_call(mix_kernel, grid=(rows // step,), in_specs=[pl.BlockSpec((...  16.6 us
    convert_element_type x6, other arithmetic, level_step(): return (own + partner).astype(jnp.bfloat16)  15.4 us
    pallas_call x1, Pallas kernels, dequant(): pl.pallas_call(dequant_kernel, grid_spec=pltpu.PrefetchScalarGridSpec(num...  14.1 us
  transfers between devices with their start and end apart: 24, of which 9 were waited for; matrix products, arithmetic and copies ran while one was open for 23% of the time, Pallas kernels for 16%

profile of v1, /device:TPU:0, one launch (start us, length us, event | category | flops | bytes accessed | tf_op | source)
XLA Modules:
  0.0 431.4 jit_solution(2533802966433765143)
XLA Ops:
  7.2 4.2 fusion.36
  11.9 2.3 copy.82
  17.4 3.5 collective-permute-start.1
  20.9 16.3 %copy.67.codes_ref = s32[5376,672]{1,0:T(8,128)} copy(s32[5376,672]{0,1:T(8,128)} %param.14) | data formatting | bytes 28901376 | tf_op args[5]
  37.2 14.1 %shard_map.92 = (bf16[256,2688]{1,0:T(8,128)(2,1)}, bf16[256,2688]{1,0:T(8,128)(2,1)}, bf16[160,2688]{1,0:T(8,128)(2,1)}) custom-call(s32[1]{0:T(128)} %bitcast.half_ref, s32[5376,672]{1,0:T(8,128)} %copy.67.codes_ref, s32[42,672]{1,0:T(8,128)} %scales_ref.1), custom_call_target="tpu_custom_call" | custom-call | flops 7225344 | bytes 14450688 | tf_op jit(solution)/shard_map/pallas_call | solution.py:264
  51.3 3.4 collective-permute-start.4
  54.8 16.6 %shard_map.91.refs_0_.refs_1_ = bf16[512,5376]{1,0:T(8,128)(2,1)} custom-call(bf16[512,5376]{1,0:T(8,128)(2,1)} %hidden_ref.1, bf16[2,1408,1408]{2,1,0:T(8,128)(2,1)} %constant.53.clone.table_ref), custom_call_target="tpu_custom_call" | custom-call | flops 7751073792 | bytes 11010048 | tf_op jit(solution)/shard_map/pallas_call | solution.py:231
  72.0 1.6 collective-permute-start.15
  73.6 1.4 fusion.8
  75.8 2.0 fusion.35
  77.8 1.8 copy.61
  79.6 1.7 copy.63
  81.3 3.9 subtract_convert_fusion
  85.2 6.2 %copy.58 = bf16[1024,2,512]{0,2,1:T(8,128)(2,1)} copy(bf16[1024,2,512]{2,1,0:T(2,128)(2,1)} %param.11) | data formatting | bytes 4194304 | tf_op args[2]
  91.4 30.7 %collective-permute-done.15 = bf16[160,2688]{1,0:T(8,128)(2,1)} collective-permute-done((bf16[160,2688]{1,0:T(8,128)(2,1)}, bf16[160,2688]{1,0:T(8,128)(2,1)}, u32[]{:S(2)}, u32[]{:S(2)}) %collective-permute-start.15) | collective-permute-done | bytes 860192 | tf_op jit(solution)/shard_map/ppermute | solution.py:389
  122.1 2.6 fusion.20
  125.4 2.1 fusion.18
  127.5 2.5 collective-permute-start.10
  131.2 1.6 collective-permute-start.2
  132.7 2.2 fusion.10
  135.0 30.1 %collective-permute-done.16 = bf16[160,2688]{1,0:T(8,128)(2,1)} collective-permute-done((bf16[160,2688]{1,0:T(8,128)(2,1)}, bf16[160,2688]{1,0:T(8,128)(2,1)}, u32[]{:S(2)}, u32[]{:S(2)}) %collective-permute-start.16) | collective-permute-done | bytes 860192 | tf_op jit(solution)/shard_map/ppermute | solution.py:389
  165.1 2.6 fusion.22.refs_6_
  167.8 1.6 collective-permute-start.17
  169.3 2.4 fusion.17
  172.0 1.4 fusion.34
  173.4 10.2 %fusion.40 = f32[4,2,512]{2,1,0:T(2,128)S(1)} fusion(pred[512,1536]{0,1:T(8,128)(4,1)} %fusion.8, bf16[1536,4,128,1]{0,2,3,1:T(8,128)(2,1)S(1)} %bitcast.51, bf16[512,4,2,64]{3,0,2,1:T(8,128)(2,1)} %bitcast.57, bf16[512,4,2,64]{3,0,2,1:T(8,128)(2,1)} %bitcast.55), kind=kOutput, calls=%fused_computation.75 | convolution fusion | flops 1637877248 | bytes 3424256 | tf_op jit(solution)/shard_map/sub | solution.py:378
  183.6 13.5 %fusion.24 = f32[4,1536,512,2]{2,1,3,0:T(8,128)} fusion(bf16[1536,4,128,1]{0,2,3,1:T(8,128)(2,1)S(1)} %bitcast.52, bf16[512,4,2,64]{3,0,2,1:T(8,128)(2,1)} %bitcast.58, bf16[512,4,2,64]{3,0,2,1:T(8,128)(2,1)} %bitcast.56), kind=kOutput, calls=%fused_computation.59 | convolution fusion | flops 1612709888 | bytes 27787264 | tf_op jit(solution)/shard_map/qkgd,skd->kgqs/dot_general | solution.py:370
  197.1 13.9 %fusion.23 = bf16[4,128,2,512]{3,1,2,0:T(8,128)(2,1)S(1)} fusion(bf16[1536,4,128,1]{0,2,3,1:T(8,128)(2,1)} %bitcast.60, f32[4,2,512]{2,1,0:T(2,128)S(1)} %fusion.40, f32[4,1536,512,2]{2,1,3,0:T(8,128)} %fusion.24, pred[512,1536]{0,1:T(8,128)(4,1)} %fusion.8), kind=kOutput, calls=%fused_computation.40 | convolution fusion | flops 1642599936 | bytes 28590080 | tf_op jit(solution)/shard_map/kgqs,skd->qkgd/dot_general | solution.py:382
  211.5 33.8 %collective-permute-start.18 = (bf16[160,2688]{1,0:T(8,128)(2,1)}, bf16[160,2688]{1,0:T(8,128)(2,1)}, u32[]{:S(2)}, u32[]{:S(2)}) collective-permute-start(bf16[160,2688]{1,0:T(8,128)(2,1)} %fusion.22.refs_6_), channel_id=1, source_target_pairs={{0,4},{4,0},{8,12},{12,8},{1,5},{5,1},{9,13},{13,9},{2,6},{6,2},{1... | collective-permute-start | bytes 2580488 | tf_op jit(solution)/shard_map/ppermute | solution.py:389
  245.4 2.2 fusion.12.refs_6_
  247.7 2.9 collective-permute-start.3
  251.1 3.4 fusion.14
  254.9 2.6 copy.68.refs_8_
  257.5 2.6 copy.69.refs_11_
  260.0 14.1 %collective-permute-done.3.refs_5_ = bf16[512,1024]{1,0:T(8,128)(2,1)S(1)} collective-permute-done((bf16[512,1024]{1,0:T(8,128)(2,1)S(1)}, bf16[512,1024]{1,0:T(8,128)(2,1)S(1)}, u32[]{:S(2)}, u32[]{:S(2)}) %collective-permute-start.3) | collective-permute-done | bytes 1048608 | tf_op jit(solution)/shard_map/ppermute | solution.py:389
  274.1 8.6 %collective-permute-done.6.refs_7_ = bf16[256,2688]{1,0:T(8,128)(2,1)} collective-permute-done((bf16[256,2688]{1,0:T(8,128)(2,1)S(1)}, bf16[256,2688]{1,0:T(8,128)(2,1)}, u32[]{:S(2)}, u32[]{:S(2)}) %collective-permute-start.6) | collective-permute-done | bytes 1376288 | tf_op jit(solution)/shard_map/ppermute | solution.py:389
  282.7 12.3 %shard_map.95 = bf16[2,1024,160]{2,1,0:T(8,128)(2,1)} custom-call(s32[1]{0:T(128)} %bitcast.half_ref, bf16[512,5376]{1,0:T(8,128)(2,1)} %shard_map.91.refs_0_.refs_1_, bf16[512,5376]{1,0:T(8,128)(2,1)} %shard_map.91.refs_0_.refs_1_, bf16[512,5376]{1,0:T(8,128)(2,1)} %collective-permute-done.refs_2_.refs_3_, ...), custom_call_target="tpu_custom_call" | custom-call | flops 4194304000 | bytes 17203200 | tf_op jit(solution)/shard_map/pallas_call | solution.py:315
  295.1 38.7 %collective-permute-done.11 = bf16[256,2688]{1,0:T(8,128)(2,1)} collective-permute-done((bf16[256,2688]{1,0:T(8,128)(2,1)}, bf16[256,2688]{1,0:T(8,128)(2,1)}, u32[]{:S(2)}, u32[]{:S(2)}) %collective-permute-start.11) | collective-permute-done | bytes 1376288 | tf_op jit(solution)/shard_map/ppermute | solution.py:389
  333.8 2.2 fusion.16.refs_6_
  336.0 1.6 collective-permute-start.12
  337.6 13.3 %shard_map.93 = bf16[2,1024,256]{2,1,0:T(8,128)(2,1)} custom-call(s32[1]{0:T(128)} %bitcast.half_ref, bf16[512,5376]{1,0:T(8,128)(2,1)} %shard_map.91.refs_0_.refs_1_, bf16[512,5376]{1,0:T(8,128)(2,1)} %shard_map.91.refs_0_.refs_1_, bf16[512,5376]{1,0:T(8,128)(2,1)} %collective-permute-done.refs_2_.refs_3_, ...), custom_call_target="tpu_custom_call" | custom-call | flops 6710886400 | bytes 19660800 | tf_op jit(solution)/shard_map/pallas_call | solution.py:315
  351.1 16.2 %collective-permute-done.12.refs_7_ = bf16[256,2688]{1,0:T(8,128)(2,1)} collective-permute-done((bf16[256,2688]{1,0:T(8,128)(2,1)S(1)}, bf16[256,2688]{1,0:T(8,128)(2,1)}, u32[]{:S(2)}, u32[]{:S(2)}) %collective-permute-start.12) | collective-permute-done | bytes 1376288 | tf_op jit(solution)/shard_map/ppermute | solution.py:389
  367.3 3.3 collective-permute-done.14.refs_10_
  371.8 13.1 %shard_map.94 = bf16[2,1024,256]{2,1,0:T(8,128)(2,1)} custom-call(s32[1]{0:T(128)} %bitcast.half_ref, bf16[512,5376]{1,0:T(8,128)(2,1)} %shard_map.91.refs_0_.refs_1_, bf16[512,5376]{1,0:T(8,128)(2,1)} %shard_map.91.refs_0_.refs_1_, bf16[512,5376]{1,0:T(8,128)(2,1)} %collective-permute-done.refs_2_.refs_3_, ...), custom_call_target="tpu_custom_call" | custom-call | flops 6710886400 | bytes 19660800 | tf_op jit(solution)/shard_map/pallas_call | solution.py:315
  386.9 24.3 %reduce-scatter.6.cloned.1.call-done = bf16[2,256,256]{2,1,0:T(8,128)(2,1)} async-done(((bf16[2,1024,256]{2,1,0:T(8,128)(2,1)}), bf16[2,256,256]{2,1,0:T(8,128)(2,1)}) %reduce-scatter.6.cloned.1.call-update) | async-done | bytes 262160 | tf_op jit(solution)/shard_map/reduce_scatter | solution.py:428
  412.2 1.6 collective-permute-start.20
  413.8 9.2 %collective-permute-done.20 = bf16[2,128,672]{2,1,0:T(8,128)(2,1)S(1)} collective-permute-done((bf16[2,128,672]{2,1,0:T(8,128)(2,1)S(1)}, bf16[2,128,672]{2,1,0:T(8,128)(2,1)S(1)}, u32[]{:S(2)}, u32[]{:S(2)}) %collective-permute-start.20) | collective-permute-done | bytes 344096 | tf_op jit(solution)/shard_map/ppermute | solution.py:389
  423.2 1.2 concatenate.44
  (84 shorter events, 13.2 us)
Async XLA Ops:
  6.5 378.3 %reduce-scatter.8.cloned.1.call-start = ((), (), s32[]{:S(2)}) async-start(), calls=%async_computation.5 | async-start | bytes 1310720 | tf_op jit(solution)/shard_map/reduce_scatter | solution.py:428
  14.2 3.2 copy-start.6
  14.8 0.7 copy-start.13
  14.8 0.7 copy-start.14
  15.5 0.8 copy-start.8
  17.4 110.1 %collective-permute-start.1 = (bf16[512,2,512]{0,2,1:T(8,128)(2,1)}, bf16[512,2,512]{0,2,1:T(8,128)(2,1)}, u32[]{:S(2)}, u32[]{:S(2)}) collective-permute-start(bf16[512,2,512]{0,2,1:T(8,128)(2,1)} %pad_maximum_fusion), channel_id=1, source_target_pairs={{0,4},{4,8},{8,12},{1,5},{5,9},{9,13},{2,6},{6,10},{10,14},{3,7},{... | collective-permute-start | bytes 3145736 | tf_op jit(solution)/shard_map/ppermute | solution.py:23
  51.3 23.7 %copy-start.15 = (bf16[512,1024]{1,0:T(8,128)(2,1)S(1)}, bf16[512,1024]{1,0:T(8,128)(2,1)}, u32[]{:S(2)}) copy-start(bf16[512,1024]{1,0:T(8,128)(2,1)} %param.9) | copy-start | bytes 3145732
  51.3 78.7 %collective-permute-start.4 = (bf16[256,2688]{1,0:T(8,128)(2,1)}, bf16[256,2688]{1,0:T(8,128)(2,1)S(1)}, u32[]{:S(2)}, u32[]{:S(2)}) collective-permute-start(bf16[256,2688]{1,0:T(8,128)(2,1)} %get-tuple-element.8), channel_id=1, source_target_pairs={{0,2},{1,3},{2,0},{3,1},{4,6},{5,7},{6,4},{7,5},{8,10},{9,11},{10,... | collective-permute-start | bytes 4128776 | tf_op jit(solution)/shard_map/ppermute | solution.py:389
  71.3 211.3 %collective-permute-start = (bf16[512,5376]{1,0:T(8,128)(2,1)}, bf16[512,5376]{1,0:T(8,128)(2,1)}, u32[]{:S(2)}, u32[]{:S(2)}) collective-permute-start(bf16[512,5376]{1,0:T(8,128)(2,1)} %shard_map.91.refs_0_.refs_1_), channel_id=1, source_target_pairs={{0,8},{4,12},{8,0},{12,4},{1,9},{5,13},{9,1},{13,5},{2,10},{6,14},... | collective-permute-start | bytes 16515080 | tf_op jit(solution)/shard_map/ppermute | solution.py:389
  72.0 175.6 %collective-permute-start.9 = (bf16[1024,672]{0,1:T(8,128)(2,1)}, bf16[1024,672]{0,1:T(8,128)(2,1)}, u32[]{:S(2)}, u32[]{:S(2)}) collective-permute-start(bf16[1024,672]{0,1:T(8,128)(2,1)} %param.16), channel_id=1, source_target_pairs={{0,4},{4,0},{8,12},{12,8},{1,5},{5,1},{9,13},{13,9},{2,6},{6,2},{1... | collective-permute-start | bytes 4128776 | tf_op jit(solution)/shard_map/ppermute | solution.py:389
  72.0 50.0 %collective-permute-start.15 = (bf16[160,2688]{1,0:T(8,128)(2,1)}, bf16[160,2688]{1,0:T(8,128)(2,1)}, u32[]{:S(2)}, u32[]{:S(2)}) collective-permute-start(bf16[160,2688]{1,0:T(8,128)(2,1)} %get-tuple-element.10), channel_id=1, source_target_pairs={{0,1},{1,0},{2,3},{3,2},{4,5},{5,4},{6,7},{7,6},{8,9},{9,8},{10,11... | collective-permute-start | bytes 2580488 | tf_op jit(solution)/shard_map/ppermute | solution.py:389
  91.4 34.0 %copy-start.2 = (bf16[1024,2,512]{0,2,1:T(8,128)(2,1)S(1)}, bf16[1024,2,512]{0,2,1:T(8,128)(2,1)}, u32[]{:S(2)}) copy-start(bf16[1024,2,512]{0,2,1:T(8,128)(2,1)} %copy.58) | copy-start | bytes 6291460
  124.7 40.4 %collective-permute-start.16 = (bf16[160,2688]{1,0:T(8,128)(2,1)}, bf16[160,2688]{1,0:T(8,128)(2,1)}, u32[]{:S(2)}, u32[]{:S(2)}) collective-permute-start(bf16[160,2688]{1,0:T(8,128)(2,1)} %fusion.20), channel_id=1, source_target_pairs={{0,2},{1,3},{2,0},{3,1},{4,6},{5,7},{6,4},{7,5},{8,10},{9,11},{10,... | collective-permute-start | bytes 2580488 | tf_op jit(solution)/shard_map/ppermute | solution.py:389
  127.5 123.0 %collective-permute-start.10 = (bf16[256,2688]{1,0:T(8,128)(2,1)}, bf16[256,2688]{1,0:T(8,128)(2,1)}, u32[]{:S(2)}, u32[]{:S(2)}) collective-permute-start(bf16[256,2688]{1,0:T(8,128)(2,1)} %get-tuple-element.9), channel_id=1, source_target_pairs={{0,1},{1,0},{2,3},{3,2},{4,5},{5,4},{6,7},{7,6},{8,9},{9,8},{10,11... | collective-permute-start | bytes 4128776 | tf_op jit(solution)/shard_map/ppermute | solution.py:389
  130.1 1.1 copy-start.12
  131.2 36.6 %collective-permute-start.2 = (bf16[512,2,512]{0,2,1:T(8,128)(2,1)}, bf16[512,2,512]{0,2,1:T(8,128)(2,1)S(1)}, u32[]{:S(2)}, u32[]{:S(2)}) collective-permute-start(bf16[512,2,512]{0,2,1:T(8,128)(2,1)} %collective-permute-done.1), channel_id=1, source_target_pairs={{0,4},{4,8},{8,12},{1,5},{5,9},{9,13},{2,6},{6,10},{10,14},{3,7},{... | collective-permute-start | bytes 3145736 | tf_op jit(solution)/shard_map/ppermute | solution.py:23
  135.0 36.8 %copy-start.5 = (bf16[256,2688]{1,0:T(8,128)(2,1)}, bf16[256,2688]{1,0:T(8,128)(2,1)S(1)}, u32[]{:S(2)}) copy-start(bf16[256,2688]{1,0:T(8,128)(2,1)S(1)} %fusion.10) | copy-start | bytes 4128772
  165.1 46.4 %collective-permute-start.5 = (bf16[256,2688]{1,0:T(8,128)(2,1)S(1)}, bf16[256,2688]{1,0:T(8,128)(2,1)}, u32[]{:S(2)}, u32[]{:S(2)}) collective-permute-start(bf16[256,2688]{1,0:T(8,128)(2,1)S(1)} %fusion.10), channel_id=1, source_target_pairs={{0,1},{1,0},{2,3},{3,2},{4,5},{5,4},{6,7},{7,6},{8,9},{9,8},{10,11... | collective-permute-start | bytes 4128776 | tf_op jit(solution)/shard_map/ppermute | solution.py:389
  167.8 4.0 copy-start.7
  167.8 4.0 copy-start.9
  167.8 86.7 %collective-permute-start.17 = (bf16[160,2688]{1,0:T(8,128)(2,1)}, bf16[160,2688]{1,0:T(8,128)(2,1)}, u32[]{:S(2)}, u32[]{:S(2)}) collective-permute-start(bf16[160,2688]{1,0:T(8,128)(2,1)} %fusion.22.refs_6_), channel_id=1, source_target_pairs={{0,16},{16,0},{1,17},{17,1},{2,18},{18,2},{3,19},{19,3},{4,20},{20... | collective-permute-start | bytes 2580488 | tf_op jit(solution)/shard_map/ppermute | solution.py:389
  211.5 43.0 %copy-start = (bf16[512,1024]{1,0:T(8,128)(2,1)}, bf16[512,1024]{1,0:T(8,128)(2,1)S(1)}, u32[]{:S(2)}) copy-start(bf16[512,1024]{1,0:T(8,128)(2,1)S(1)} %copy.79.refs_4_) | copy-start | bytes 3145732
  211.5 43.3 %collective-permute-start.18 = (bf16[160,2688]{1,0:T(8,128)(2,1)}, bf16[160,2688]{1,0:T(8,128)(2,1)}, u32[]{:S(2)}, u32[]{:S(2)}) collective-permute-start(bf16[160,2688]{1,0:T(8,128)(2,1)} %fusion.22.refs_6_), channel_id=1, source_target_pairs={{0,4},{4,0},{8,12},{12,8},{1,5},{5,1},{9,13},{13,9},{2,6},{6,2},{1... | collective-permute-start | bytes 2580488 | tf_op jit(solution)/shard_map/ppermute | solution.py:389
  247.6 26.4 %copy-start.3 = (bf16[256,2688]{1,0:T(8,128)(2,1)}, bf16[256,2688]{1,0:T(8,128)(2,1)S(1)}, u32[]{:S(2)}) copy-start(bf16[256,2688]{1,0:T(8,128)(2,1)S(1)} %fusion.12.refs_6_) | copy-start | bytes 4128772
  247.7 26.4 %collective-permute-start.3 = (bf16[512,1024]{1,0:T(8,128)(2,1)S(1)}, bf16[512,1024]{1,0:T(8,128)(2,1)S(1)}, u32[]{:S(2)}, u32[]{:S(2)}) collective-permute-start(bf16[512,1024]{1,0:T(8,128)(2,1)S(1)} %copy.79.refs_4_), channel_id=1, source_target_pairs={{0,8},{4,12},{8,0},{12,4},{1,9},{5,13},{9,1},{13,5},{2,10},{6,14},... | collective-permute-start | bytes 3145736 | tf_op jit(solution)/shard_map/ppermute | solution.py:389
  250.5 32.1 %collective-permute-start.6 = (bf16[256,2688]{1,0:T(8,128)(2,1)S(1)}, bf16[256,2688]{1,0:T(8,128)(2,1)}, u32[]{:S(2)}, u32[]{:S(2)}) collective-permute-start(bf16[256,2688]{1,0:T(8,128)(2,1)S(1)} %fusion.12.refs_6_), channel_id=1, source_target_pairs={{0,16},{16,0},{1,17},{17,1},{2,18},{18,2},{3,19},{19,3},{4,20},{20... | collective-permute-start | bytes 4128776 | tf_op jit(solution)/shard_map/ppermute | solution.py:389
  254.5 79.3 %collective-permute-start.11 = (bf16[256,2688]{1,0:T(8,128)(2,1)}, bf16[256,2688]{1,0:T(8,128)(2,1)}, u32[]{:S(2)}, u32[]{:S(2)}) collective-permute-start(bf16[256,2688]{1,0:T(8,128)(2,1)} %fusion.14), channel_id=1, source_target_pairs={{0,2},{1,3},{2,0},{3,1},{4,6},{5,7},{6,4},{7,5},{8,10},{9,11},{10,... | collective-permute-start | bytes 4128776 | tf_op jit(solution)/shard_map/ppermute | solution.py:389
  254.9 27.8 %collective-permute-start.19 = (bf16[160,2688]{1,0:T(8,128)(2,1)}, bf16[160,2688]{1,0:T(8,128)(2,1)}, u32[]{:S(2)}, u32[]{:S(2)}) collective-permute-start(bf16[160,2688]{1,0:T(8,128)(2,1)} %collective-permute-done.17.refs_7_), channel_id=1, source_target_pairs={{0,4},{4,0},{8,12},{12,8},{1,5},{5,1},{9,13},{13,9},{2,6},{6,2},{1... | collective-permute-start | bytes 2580488 | tf_op jit(solution)/shard_map/ppermute | solution.py:389
  274.1 8.6 %copy-start.1 = (bf16[512,1024]{1,0:T(8,128)(2,1)}, bf16[512,1024]{1,0:T(8,128)(2,1)S(1)}, u32[]{:S(2)}) copy-start(bf16[512,1024]{1,0:T(8,128)(2,1)S(1)} %collective-permute-done.3.refs_5_) | copy-start | bytes 3145732
  274.1 63.5 %collective-permute-start.7 = (bf16[256,2688]{1,0:T(8,128)(2,1)S(1)}, bf16[256,2688]{1,0:T(8,128)(2,1)}, u32[]{:S(2)}, u32[]{:S(2)}) collective-permute-start(bf16[256,2688]{1,0:T(8,128)(2,1)S(1)} %fusion.12.refs_6_), channel_id=1, source_target_pairs={{0,4},{4,0},{8,12},{12,8},{1,5},{5,1},{9,13},{13,9},{2,6},{6,2},{1... | collective-permute-start | bytes 4128776 | tf_op jit(solution)/shard_map/ppermute | solution.py:389
  282.7 54.9 %collective-permute-start.8 = (bf16[256,2688]{1,0:T(8,128)(2,1)}, bf16[256,2688]{1,0:T(8,128)(2,1)}, u32[]{:S(2)}, u32[]{:S(2)}) collective-permute-start(bf16[256,2688]{1,0:T(8,128)(2,1)} %collective-permute-done.6.refs_7_), channel_id=1, source_target_pairs={{0,4},{4,0},{8,12},{12,8},{1,5},{5,1},{9,13},{13,9},{2,6},{6,2},{1... | collective-permute-start | bytes 4128776 | tf_op jit(solution)/shard_map/ppermute | solution.py:389
  295.1 90.8 %reduce-scatter.4.cloned.1.call-start = ((), (), s32[]{:S(2)}) async-start(), calls=%async_computation.3 | async-start | bytes 1310720 | tf_op jit(solution)/shard_map/reduce_scatter | solution.py:428
  336.0 14.9 %copy-start.4 = (bf16[256,2688]{1,0:T(8,128)(2,1)}, bf16[256,2688]{1,0:T(8,128)(2,1)S(1)}, u32[]{:S(2)}) copy-start(bf16[256,2688]{1,0:T(8,128)(2,1)S(1)} %fusion.16.refs_6_) | copy-start | bytes 4128772
  336.0 31.2 %collective-permute-start.12 = (bf16[256,2688]{1,0:T(8,128)(2,1)S(1)}, bf16[256,2688]{1,0:T(8,128)(2,1)}, u32[]{:S(2)}, u32[]{:S(2)}) collective-permute-start(bf16[256,2688]{1,0:T(8,128)(2,1)S(1)} %fusion.16.refs_6_), channel_id=1, source_target_pairs={{0,16},{16,0},{1,17},{17,1},{2,18},{18,2},{3,19},{19,3},{4,20},{20... | collective-permute-start | bytes 4128776 | tf_op jit(solution)/shard_map/ppermute | solution.py:389
  350.9 60.3 %reduce-scatter.6.cloned.1.call-start = ((), (), s32[]{:S(2)}) async-start(), calls=%async_computation.4 | async-start | bytes 1310720 | tf_op jit(solution)/shard_map/reduce_scatter | solution.py:428
  351.0 16.3 %collective-permute-start.13 = (bf16[256,2688]{1,0:T(8,128)(2,1)S(1)}, bf16[256,2688]{1,0:T(8,128)(2,1)S(1)}, u32[]{:S(2)}, u32[]{:S(2)}) collective-permute-start(bf16[256,2688]{1,0:T(8,128)(2,1)S(1)} %fusion.16.refs_6_), channel_id=1, source_target_pairs={{0,4},{4,0},{8,12},{12,8},{1,5},{5,1},{9,13},{13,9},{2,6},{6,2},{1... | collective-permute-start | bytes 4128776 | tf_op jit(solution)/shard_map/ppermute | solution.py:389
  367.2 3.3 collective-permute-start.14
  367.3 3.3 copy-start.10
  370.6 1.2 copy-start.11
  412.2 10.8 %collective-permute-start.20 = (bf16[2,128,672]{2,1,0:T(8,128)(2,1)S(1)}, bf16[2,128,672]{2,1,0:T(8,128)(2,1)S(1)}, u32[]{:S(2)}, u32[]{:S(2)}) collective-permute-start(bf16[2,128,672]{2,1,0:T(8,128)(2,1)S(1)} %pad_maximum_fusion.4), channel_id=1, source_target_pairs={{0,8},{4,12},{8,0},{12,4},{1,9},{5,13},{9,1},{13,5},{2,10},{6,14},... | collective-permute-start | bytes 1032200 | tf_op jit(solution)/shard_map/ppermute | solution.py:389
Sparse Core Ops, SparseCore 0:
  295.2 32.7 reduce-scatter.7
  351.0 24.2 reduce-scatter.3
  385.0 26.1 reduce-scatter.5
